TPU v7x, 32 devices: a whole 2x2x4 slice. The times are simulated.
32 devices in a mesh: runs: 2 (over y), space: 4 (over z), sub: 2 (over x), lane: 2 (over core).
Axes of the slice: x: 2, y: 2, z: 4, core: 2. Of those that a mesh axis runs over, the one named last changes fastest.
Arguments:
- fine_moments: bfloat16 [81, 6144], P(None, ('runs', 'space', 'sub', 'lane')), parts along dimension 1, may hold values from -6 to 6
- coarse_moments: bfloat16 [81, 512], P(None, ('runs', 'space', 'sub', 'lane')), parts along dimension 1, may hold values from -12 to 12
- m2l_table: bfloat16 [158, 81, 81], replicated, may hold values from -0.078125 to 0.078125
- fine_pairs: int32 [3, 196608], P(None, ('runs', 'space', 'sub', 'lane')), parts along dimension 1, may hold values from 0 to 3071, as said below
- coarse_pairs: int32 [3, 65536], P(None, ('runs', 'space', 'sub', 'lane')), parts along dimension 1, may hold values from 0 to 255, as said below
Outputs:
- fine_local: float32 [81, 6144], P(None, ('runs', 'space', 'sub', 'lane')), parts along dimension 1
- coarse_local: float32 [81, 512], P(None, ('runs', 'space', 'sub', 'lane')), parts along dimension 1
There are 2 independent parts, one for each index of `runs`. A program takes and returns all parts, laid end to end along the dimension named above; an argument that names none is the same for every part. Nothing has to cross between parts.
Inputs may be any that keep to these rules, and one draw needn't show every extreme that they name: `fine_pairs`: row 0 holds source cells, row 1 target cells, row 2 offset classes. The 6144 slots of one device come in aligned blocks of 128 with one class each; class 158 marks an empty block, whose pairs add nothing. A device's target cells lie in its own group of 768 consecutive cells (the group of its index along space), its source cells in that group or one of the two beside it. `coarse_pairs`: row 0 holds source cells, row 1 target cells, row 2 offset classes. The 2048 slots of one device come in aligned blocks of 128 with one class each; class 158 marks an empty block. A device's target cells are among its own 16 cells; its source cells lie in its own group of 64 consecutive coarse cells (the group of its index along space) or one of the two beside it.
All inputs are finite; a program needn't handle non-finite values.
Results may differ from a plain program's by a relative error of at most 0.0003.
Values may be sent and summed in bfloat16 or wider, within the bound.
A program may use at most 64 MiB of HBM per device.

v0:
```python
import jax
import jax.numpy as jnp
from jax import lax
from jax.sharding import PartitionSpec as P

BLK = 128


def with_halo(block, sides, width):
    for axis, dim in sides:
        count = lax.axis_size(axis)
        forward = [(i, i + 1) for i in range(count - 1)]
        backward = [(target, source) for source, target in forward]
        low = lax.ppermute(
            lax.slice_in_dim(block, block.shape[dim] - width, None, axis=dim), axis, forward
        )
        high = lax.ppermute(lax.slice_in_dim(block, 0, width, axis=dim), axis, backward)
        block = jnp.concatenate([low, block, high], axis=dim)
    return block


def from_behind(shard, axis, by):
    size = lax.axis_size(axis)
    pairs = [(i, i + by) for i in range(size) if 0 <= i + by < size]
    return lax.ppermute(shard, axis, pairs)


def degree_sign(count):
    index = jnp.arange(count)
    squares = jnp.arange(1, 17) ** 2
    degree = jnp.sum((index[:, None] >= squares[None, :]).astype(jnp.int32), axis=1)
    return jnp.where(degree % 2 == 1, -1.0, 1.0).astype(jnp.float32)


def pair_terms(moments, pairs, offset, table, parity, cells):
    width = moments.shape[0]
    source = pairs[0] - offset
    target = pairs[1] - offset
    nblocks = source.shape[0] // BLK
    src_b = source.reshape(nblocks, BLK)
    tgt_b = target.reshape(nblocks, BLK)
    fetch = jnp.stack([src_b, tgt_b], axis=1).reshape(-1)
    store = jnp.stack([tgt_b, src_b], axis=1).reshape(-1)
    flips = jnp.stack([jnp.ones_like(parity), parity], axis=1)
    picked = (
        moments[:, fetch].reshape(width, nblocks, 2, BLK)
        * flips.astype(jnp.bfloat16)[:, None, :, None]
    )
    operators = table[pairs[2].reshape(nblocks, BLK)[:, 0]]
    result = jnp.einsum("bij,jbsn->ibsn", operators, picked, preferred_element_type=jnp.float32)
    result = result * flips[:, None, :, None]
    total = jnp.zeros((width, cells), jnp.float32)
    return total.at[:, store].add(result.reshape(width, -1))


def per_device(fine_moments, coarse_moments, m2l_table, fine_pairs, coarse_pairs):
    width = fine_moments.shape[0]
    parity = degree_sign(width)
    table = jnp.concatenate([m2l_table, jnp.zeros((1, width, width), jnp.bfloat16)], axis=0)
    grouped_fine, grouped_coarse = (
        lax.all_gather(fine_moments, ("sub", "lane"), axis=1, tiled=True),
        lax.all_gather(coarse_moments, ("sub", "lane"), axis=1, tiled=True),
    )
    fine_span = grouped_fine.shape[1]
    coarse_span = grouped_coarse.shape[1]
    joint = fine_span + coarse_span
    joined = jnp.concatenate([grouped_fine, grouped_coarse], axis=1)
    window = with_halo(joined, (("space", 1),), joint)
    fine_window = jnp.concatenate(
        [window[:, j * joint : j * joint + fine_span] for j in range(3)], axis=1
    )
    coarse_window = jnp.concatenate(
        [window[:, j * joint + fine_span : (j + 1) * joint] for j in range(3)], axis=1
    )
    place = lax.axis_index("space") - 1
    fine_part = pair_terms(fine_window, fine_pairs, place * fine_span, table, parity, 3 * fine_span)
    coarse_part = pair_terms(
        coarse_window, coarse_pairs, place * coarse_span, table, parity, 3 * coarse_span
    )
    lower = jnp.concatenate([fine_part[:, :fine_span], coarse_part[:, :coarse_span]], axis=1)
    upper = jnp.concatenate(
        [fine_part[:, 2 * fine_span :], coarse_part[:, 2 * coarse_span :]], axis=1
    )
    from_above = from_behind(lower, "space", -1)
    from_below = from_behind(upper, "space", 1)
    fine_mid = (
        fine_part[:, fine_span : 2 * fine_span]
        + from_above[:, :fine_span]
        + from_below[:, :fine_span]
    )
    coarse_mid = (
        coarse_part[:, coarse_span : 2 * coarse_span]
        + from_above[:, fine_span:]
        + from_below[:, fine_span:]
    )
    fine_local, coarse_local = (
        lax.psum_scatter(fine_mid, ("sub", "lane"), scatter_dimension=1, tiled=True),
        lax.psum_scatter(coarse_mid, ("sub", "lane"), scatter_dimension=1, tiled=True),
    )
    return (fine_local, coarse_local)


def solution(mesh):
    placed = (
        P(None, ("runs", "space", "sub", "lane")),
        P(None, ("runs", "space", "sub", "lane")),
        P(),
        P(None, ("runs", "space", "sub", "lane")),
        P(None, ("runs", "space", "sub", "lane")),
    )
    return jax.shard_map(
        per_device,
        mesh=mesh,
        in_specs=placed,
        out_specs=(
            P(None, ("runs", "space", "sub", "lane")),
            P(None, ("runs", "space", "sub", "lane")),
        ),
        check_vma=False,
    )
```

profile of v0, /device:TPU:13, one launch (start us, length us, event | category | flops | bytes accessed | tf_op | source)
XLA Modules:
  0.0 278.4 jit_solution(12918364982083327676)
XLA Ops:
  7.2 0.0 reduce-scatter.3.cloned.1.call-start
  7.2 5.8 %all_gather.7 = bf16[81,64]{0,1:T(8,128)(2,1)S(1)} all-gather(bf16[81,16]{0,1:T(8,128)(2,1)} %param.6), channel_id=1, replica_groups=mesh['runs'=2,'space'=4,'sub'=2,'lane'=2] {'sub','lane'}, dimensions={1}, use_global_device_ids=true | all-gather | bytes 12960 | tf_op jit(solution)/shard_map/all_gather | solution.py:62
  13.0 5.8 %all-gather = bf16[4,192,81]{1,2,0:T(8,128)(2,1)S(1)} all-gather(bf16[1,192,81]{1,2,0:T(8,128)(2,1)} %bitcast.82), channel_id=1, replica_groups=mesh['runs'=2,'space'=4,'sub'=2,'lane'=2] {'sub','lane'}, dimensions={0}, use_global_device_ids=true | all-gather | bytes 155520 | tf_op jit(solution)/shard_map/all_gather | solution.py:61
  18.8 0.2 copy.55
  19.0 2.1 collective-permute-start.1
  21.1 3.2 %collective-permute-start = (bf16[81,832]{0,1:T(8,128)(2,1)S(1)}, bf16[81,832]{0,1:T(8,128)(2,1)S(1)}, u32[]{:S(2)}, u32[]{:S(2)}) collective-permute-start(bf16[81,832]{0,1:T(8,128)(2,1)S(1)} %pad_maximum_fusion.3), channel_id=1, source_target_pairs={{0,4},{4,8},{8,12},{1,5},{5,9},{9,13},{2,6},{6,10},{10,14},{3,7},{... | collective-permute-start | bytes 404360 | tf_op jit(solution)/shard_map/ppermute | solution.py:14
  24.3 0.1 convert_reduce_fusion
  24.4 0.9 fusion.17
  25.3 0.1 copy.75
  25.5 1.1 fusion.16
  26.7 0.1 copy.74
  26.7 0.1 pad_add_fusion.1
  26.8 0.1 compare_select_fusion
  26.9 0.1 compare_select_fusion.1
  27.0 3.3 %copy.59 = bf16[158,81,81]{2,1,0:T(8,128)(2,1)S(1)} copy(bf16[158,81,81]{2,0,1:T(8,128)(2,1)} %param.7) | data formatting | bytes 4146552 | tf_op args[2]
  30.2 2.5 concatenate.20
  32.7 2.6 gather_fusion.3
  35.3 3.7 %gather_fusion.1 = bf16[48,81,81]{2,1,0:T(8,128)(2,1)} fusion(bf16[159,81,81]{2,1,0:T(8,128)(2,1)} %concatenate.20, s32[1024]{0:T(1024)S(1)} %pad_clamp_fusion.1), kind=kCustom, calls=%fused_computation.1 | custom fusion | bytes 1259904 | tf_op jit(solution)/shard_map/gather | solution.py:49
  39.1 0.0 copy-start.1
  39.1 0.0 copy-start.3
  39.1 0.0 collective-permute-done.1
  39.1 0.0 collective-permute-done
  39.2 12.1 %gather_fusion.2 = bf16[4096,81]{1,0:T(8,128)(2,1)S(1)} fusion(bf16[81,192]{0,1:T(8,128)(2,1)S(1)} %pad_maximum_fusion.4, s32[4096]{0:T(1024)S(1)} %broadcast_clamp_fusion.1), kind=kCustom, calls=%fused_computation.2 | custom fusion | bytes 1343488 | tf_op jit(solution)/shard_map/gather | solution.py:46
  51.3 0.6 copy.67
  52.0 0.1 pad_maximum_fusion
  52.1 43.6 %gather_fusion = bf16[12288,81]{1,0:T(8,128)(2,1)} fusion(bf16[81,2304]{0,1:T(8,128)(2,1)S(1)} %pad_maximum_fusion, s32[12288]{0:T(1024)S(1)} %broadcast_clamp_fusion), kind=kCustom, calls=%fused_computation | custom fusion | bytes 4030464 | tf_op jit(solution)/shard_map/gather | solution.py:46
  95.8 3.4 %copy.58 = bf16[81,48,2,128]{3,0,2,1:T(8,128)(2,1)S(1)} copy(bf16[81,48,2,128]{0,3,2,1:T(8,128)(2,1)} %bitcast.69) | data formatting | bytes 3981312 | tf_op jit(solution)/shard_map/reshape | solution.py:46
  99.2 0.0 copy-done.1
  99.2 0.0 copy-done.3
  99.2 0.4 fusion.1
  99.7 0.7 copy.69
  100.4 2.2 reshape.287
  102.5 0.0 copy-start
  102.5 0.0 copy-start.2
  102.5 0.0 copy-start.4
  102.5 3.0 %copy.70 = f32[4096,81]{1,0:T(8,128)} copy(f32[4096,81]{0,1:T(8,128)} %bitcast.70) | data formatting | bytes 2654208 | tf_op jit(solution)/shard_map/reshape | solution.py:53
  105.5 22.9 %scatter_custom_fusion.1 = f32[81,192]{0,1:T(8,128)S(1)} fusion(s32[4096]{0:T(1024)S(1)} %bitcast.84, f32[4096,81]{1,0:T(8,128)} %copy.70, f32[]{:T(128)} %constant.15.clone.1), kind=kCustom, calls=%fused_computation.30 | custom fusion | flops 331776 | bytes 62720 | tf_op jit(solution)/shard_map/scatter-add | solution.py:53
  128.4 0.0 copy-done
  128.4 0.0 copy-done.2
  128.4 0.0 copy-done.4
  128.4 0.8 bitcast_multiply_fusion
  129.2 3.9 %copy.61 = f32[81,48,2,128]{3,2,1,0:T(2,128)} copy(f32[81,48,2,128]{3,0,2,1:T(8,128)S(1)} %bitcast_multiply_fusion) | data formatting | bytes 7962624 | tf_op jit(solution)/shard_map/mul | solution.py:51
  133.1 6.3 %reshape.279 = f32[81,12288]{1,0:T(8,128)} reshape(f32[81,48,2,128]{3,2,1,0:T(2,128)} %copy.61) | data formatting | bytes 7962624 | tf_op jit(solution)/shard_map/reshape | solution.py:53
  139.4 6.2 %copy.62 = f32[12288,81]{1,0:T(8,128)} copy(f32[12288,81]{0,1:T(8,128)} %bitcast.68) | data formatting | bytes 7962624 | tf_op jit(solution)/shard_map/reshape | solution.py:53
  145.6 66.3 %scatter_custom_fusion = f32[81,2304]{0,1:T(8,128)S(1)} fusion(s32[12288]{0:T(1024)S(1)} %bitcast.81, f32[12288,81]{1,0:T(8,128)} %copy.62, f32[]{:T(128)} %constant.15.clone.1), kind=kCustom, calls=%fused_computation.14 | custom fusion | flops 995328 | bytes 747008 | tf_op jit(solution)/shard_map/scatter-add | solution.py:53
  211.9 0.1 fusion.14
  212.0 3.2 %collective-permute-start.3 = (f32[81,832]{0,1:T(8,128)S(1)}, f32[81,832]{0,1:T(8,128)S(1)}, u32[]{:S(2)}, u32[]{:S(2)}) collective-permute-start(f32[81,832]{0,1:T(8,128)S(1)} %pad_maximum_fusion.2), channel_id=1, source_target_pairs={{0,4},{4,8},{8,12},{1,5},{5,9},{9,13},{2,6},{6,10},{10,14},{3,7},{... | collective-permute-start | bytes 808712 | tf_op jit(solution)/shard_map/ppermute | solution.py:25
  215.3 2.1 collective-permute-start.2
  217.4 7.1 %collective-permute-done.3 = f32[81,832]{0,1:T(8,128)S(1)} collective-permute-done((f32[81,832]{0,1:T(8,128)S(1)}, f32[81,832]{0,1:T(8,128)S(1)}, u32[]{:S(2)}, u32[]{:S(2)}) %collective-permute-start.3) | collective-permute-done | bytes 269600 | tf_op jit(solution)/shard_map/ppermute | solution.py:25
  224.5 3.0 %collective-permute-done.2 = f32[81,832]{0,1:T(8,128)S(1)} collective-permute-done((f32[81,832]{0,1:T(8,128)S(1)}, f32[81,832]{0,1:T(8,128)S(1)}, u32[]{:S(2)}, u32[]{:S(2)}) %collective-permute-start.2) | collective-permute-done | bytes 269600 | tf_op jit(solution)/shard_map/ppermute | solution.py:25
  227.5 0.8 slice_add_fusion
  228.3 0.0 reduce-scatter.3.cloned.1.call-update
  228.3 0.0 reduce-scatter.5.cloned.1.call-start
  228.4 0.6 slice_add_fusion.2
  229.0 0.1 reduce-scatter.5.cloned.1.call-update
  229.1 20.5 %reduce-scatter.3.cloned.1.call-done = f32[81,192]{0,1:T(8,128)} async-done(((f32[81,768]{0,1:T(8,128)}), f32[81,192]{0,1:T(8,128)}) %reduce-scatter.3.cloned.1.call-update) | async-done | bytes 62224 | tf_op jit(solution)/shard_map/reduce_scatter | solution.py:97
  249.6 1.6 copy.71
  251.2 20.3 %reduce-scatter.5.cloned.1.call-done = f32[81,16]{0,1:T(8,128)} async-done(((f32[81,64]{0,1:T(8,128)}), f32[81,16]{0,1:T(8,128)}) %reduce-scatter.5.cloned.1.call-update) | async-done | bytes 5200 | tf_op jit(solution)/shard_map/reduce_scatter | solution.py:98
  (22 shorter events, 0.3 us)
Async XLA Ops:
  7.2 242.4 %reduce-scatter.3.cloned.1.call-start = ((), (), s32[]{:S(2)}) async-start(), calls=%async_computation.2 | async-start | bytes 491520 | tf_op jit(solution)/shard_map/reduce_scatter | solution.py:97
  19.0 20.1 %collective-permute-start.1 = (bf16[81,832]{0,1:T(8,128)(2,1)S(1)}, bf16[81,832]{0,1:T(8,128)(2,1)S(1)}, u32[]{:S(2)}, u32[]{:S(2)}) collective-permute-start(bf16[81,832]{0,1:T(8,128)(2,1)S(1)} %pad_maximum_fusion.3), channel_id=1, source_target_pairs={{4,0},{8,4},{12,8},{5,1},{9,5},{13,9},{6,2},{10,6},{14,10},{7,3},{... | collective-permute-start | bytes 404360 | tf_op jit(solution)/shard_map/ppermute | solution.py:17
  21.1 18.0 %collective-permute-start = (bf16[81,832]{0,1:T(8,128)(2,1)S(1)}, bf16[81,832]{0,1:T(8,128)(2,1)S(1)}, u32[]{:S(2)}, u32[]{:S(2)}) collective-permute-start(bf16[81,832]{0,1:T(8,128)(2,1)S(1)} %pad_maximum_fusion.3), channel_id=1, source_target_pairs={{0,4},{4,8},{8,12},{1,5},{5,9},{9,13},{2,6},{6,10},{10,14},{3,7},{... | collective-permute-start | bytes 404360 | tf_op jit(solution)/shard_map/ppermute | solution.py:14
  39.1 60.1 %copy-start.1 = (f32[81,2]{0,1:T(2,128)}, f32[81,2]{0,1:T(2,128)S(1)}, u32[]{:S(2)}) copy-start(f32[81,2]{0,1:T(2,128)S(1)} %stack.20) | copy-start | bytes 1948
  39.1 60.1 %copy-start.3 = (bf16[81,2]{0,1:T(2,128)(2,1)}, bf16[81,2]{0,1:T(2,128)(2,1)S(1)}, u32[]{:S(2)}) copy-start(bf16[81,2]{0,1:T(2,128)(2,1)S(1)} %pad_convert_fusion) | copy-start | bytes 976
  102.5 25.9 %copy-start = (bf16[48,81,81]{2,1,0:T(8,128)(2,1)S(1)}, bf16[48,81,81]{2,1,0:T(8,128)(2,1)}, u32[]{:S(2)}) copy-start(bf16[48,81,81]{2,1,0:T(8,128)(2,1)} %gather_fusion.1) | copy-start | bytes 1889572
  102.5 25.9 %copy-start.2 = (f32[81,2]{0,1:T(2,128)S(1)}, f32[81,2]{0,1:T(2,128)}, u32[]{:S(2)}) copy-start(f32[81,2]{0,1:T(2,128)} %copy-done.1) | copy-start | bytes 1948
  102.5 25.9 %copy-start.4 = (bf16[81,2]{0,1:T(2,128)(2,1)S(1)}, bf16[81,2]{0,1:T(2,128)(2,1)}, u32[]{:S(2)}) copy-start(bf16[81,2]{0,1:T(2,128)(2,1)} %copy-done.3) | copy-start | bytes 976
  212.0 12.5 %collective-permute-start.3 = (f32[81,832]{0,1:T(8,128)S(1)}, f32[81,832]{0,1:T(8,128)S(1)}, u32[]{:S(2)}, u32[]{:S(2)}) collective-permute-start(f32[81,832]{0,1:T(8,128)S(1)} %pad_maximum_fusion.2), channel_id=1, source_target_pairs={{0,4},{4,8},{8,12},{1,5},{5,9},{9,13},{2,6},{6,10},{10,14},{3,7},{... | collective-permute-start | bytes 808712 | tf_op jit(solution)/shard_map/ppermute | solution.py:25
  215.3 12.2 %collective-permute-start.2 = (f32[81,832]{0,1:T(8,128)S(1)}, f32[81,832]{0,1:T(8,128)S(1)}, u32[]{:S(2)}, u32[]{:S(2)}) collective-permute-start(f32[81,832]{0,1:T(8,128)S(1)} %pad_maximum_fusion.1), channel_id=1, source_target_pairs={{4,0},{8,4},{12,8},{5,1},{9,5},{13,9},{6,2},{10,6},{14,10},{7,3},{... | collective-permute-start | bytes 808712 | tf_op jit(solution)/shard_map/ppermute | solution.py:25
  228.3 43.2 %reduce-scatter.5.cloned.1.call-start = ((), (), s32[]{:S(2)}) async-start(), calls=%async_computation.3 | async-start | bytes 40960 | tf_op jit(solution)/shard_map/reduce_scatter | solution.py:98
Sparse Core Ops, SparseCore 0:
  228.4 21.1 reduce-scatter.2
  252.6 18.8 reduce-scatter.4
where the time goes:
time: 281 us; the launch traced here: 278 us
  local copies, waits for them, and re-layouts  96.2 us (34%)
  other arithmetic  93.2 us (33%)
  waiting for transfers between devices  51 us (18%)
  between operations  14.4 us (5%)
  blocking collectives  11.6 us (4%)
  starting transfers between devices  10.7 us (4%)
    scatter-add x2, other arithmetic, pair_terms(): return total.at[:, store].add(result.reshape(width, -1))  89.1 us
    gather x2, local copies, waits for them, and re-layouts, pair_terms(): moments[:, fetch].reshape(width, nblocks, 2, BLK)  55.8 us
    reduce_scatter x1, waiting for transfers between devices, per_device(): lax.psum_scatter(fine_mid, ('sub', 'lane'), scatter_dimension=1, tiled=True)  20.5 us
    reduce_scatter x1, waiting for transfers between devices, per_device(): lax.psum_scatter(coarse_mid, ('sub', 'lane'), scatter_dimension=1, tiled=...  20.3 us
    reshape x4, local copies, waits for them, and re-layouts, pair_terms(): return total.at[:, store].add(result.reshape(width, -1))  17.6 us
    ppermute x2, waiting for transfers between devices, from_behind(): return lax.ppermute(shard, axis, pairs)  10.1 us
    gather x2, local copies, waits for them, and re-layouts, pair_terms(): operators = table[pairs[2].reshape(nblocks, BLK)[:, 0]]  6.37 us
    all_gather x1, blocking collectives, per_device(): lax.all_gather(fine_moments, ('sub', 'lane'), axis=1, tiled=True)  5.8 us
  transfers between devices with their start and end apart: 6, of which 4 were waited for; matrix products, arithmetic and copies ran while one was open for 6% of the time, Pallas kernels for 0%

commit v1 on v0

v1 whole, which is shorter than its diff:
```python
import functools

import jax
import jax.numpy as jnp
from jax import lax
from jax.experimental import pallas as pl
from jax.experimental.pallas import tpu as pltpu
from jax.sharding import PartitionSpec as P

BLK = 128
STEP = 256
LANES = 256
ROWS = 96
F32 = jnp.float32
BF16 = jnp.bfloat16


def divider(width, limit):
    for shift in range(31):
        mul = -(-(1 << shift) // width)
        if all((w * mul) >> shift == w // width for w in range(limit)):
            break
    assert limit * mul < 2**31
    return lambda w: (w * mul) >> shift


def row_sign(rows, dtype):
    index = lax.broadcasted_iota(jnp.int32, (rows, 1), 0)
    degree = jnp.zeros((rows, 1), jnp.int32)
    for root in range(1, 17):
        degree = degree + jnp.where(index >= root * root, 1, 0)
    return (1 - 2 * (degree & 1)).astype(F32).astype(dtype)


def split(values):
    top = values.astype(BF16)
    return top, (values - top.astype(F32)).astype(BF16)


def one_hot(lo):
    index = lax.broadcasted_iota(jnp.int32, (LANES, STEP), 0)
    return jnp.where(index == lo, 1.0, 0.0).astype(BF16)


def pick(stack, first, count, hi, hot):
    height = stack.shape[1]
    block = stack[first : first + count].reshape(count * height, LANES)
    all_parts = jnp.dot(block, hot, preferred_element_type=F32)
    got = jnp.zeros((height, STEP), F32)
    for h in range(count):
        got = jnp.where(hi == first + h, all_parts[h * height : (h + 1) * height], got)
    return got


def put(acc, first, count, hi, hot, values):
    height = values.shape[0]
    top, rest = split(values)
    both = jnp.concatenate([top, rest], axis=1)
    hi2 = jnp.concatenate([hi, hi], axis=1)
    spread = jnp.concatenate(
        [
            both * jnp.where(hi2 == first + h, 1.0, 0.0).astype(BF16)
            for h in range(count)
        ],
        axis=0,
    )
    hot2 = jnp.concatenate([hot, hot], axis=1)
    total = lax.dot_general(
        spread, hot2, (((1,), (1,)), ((), ())), preferred_element_type=F32
    )
    acc[...] += total.reshape(count, height, LANES)


def level(
    pairs, classes, table, stack, flipped, acc_src, acc_tgt, res, offset, width, mid, cells
):
    width_of = divider(width, cells)
    classes_count = table.shape[0]
    k = table.shape[1]
    src_count = stack.shape[0]
    first, tgt_count = mid

    def step(i, carry):
        base = pl.multiple_of(i * STEP, STEP)
        src = pairs[0:1, pl.ds(base, STEP)] - offset
        tgt = pairs[1:2, pl.ds(base, STEP)] - offset
        live = pairs[2:3, pl.ds(base, STEP)] < classes_count
        src_hi = width_of(src)
        tgt_hi = width_of(tgt)
        src_hot = one_hot(src - src_hi * width)
        tgt_hot = one_hot(tgt - tgt_hi * width)
        src_hi = jnp.where(live, src_hi, -1)
        tgt_hi = jnp.where(live, tgt_hi, -1)
        from_src = pick(stack, 0, src_count, src_hi, src_hot)
        from_tgt = pick(flipped, first, tgt_count, tgt_hi, tgt_hot)
        for j in range(STEP // BLK):
            at = slice(j * BLK, (j + 1) * BLK)
            operand = jnp.concatenate([from_src[:, at], from_tgt[:, at]], axis=1).astype(BF16)
            kind = jnp.minimum(classes[2, base + j * BLK], classes_count - 1)
            moved = jnp.dot(table[kind], operand[:k], preferred_element_type=F32)
            res[0, :k, at] = moved[:, :BLK]
            res[1, :k, at] = moved[:, BLK:]
        put(acc_tgt, first, tgt_count, tgt_hi, tgt_hot, res[0])
        put(acc_src, 0, src_count, src_hi, src_hot, res[1])
        return carry

    lax.fori_loop(0, pairs.shape[1] // STEP, step, 0)


def compute(
    sizes,
    fine_stack,
    coarse_stack,
    table,
    fine_pairs,
    coarse_pairs,
    fine_classes,
    coarse_classes,
    fine_out,
    coarse_out,
    fine_flip,
    coarse_flip,
    fine_tgt,
    coarse_tgt,
    res,
):
    cf, cc, members, axis = sizes
    place = lax.axis_index(axis) - 1
    sign_b = row_sign(ROWS, BF16)
    sign_f = row_sign(ROWS, F32)
    fine_flip[...] = fine_stack[...] * sign_b
    coarse_flip[...] = coarse_stack[...] * sign_b
    for ref in (fine_out, coarse_out, fine_tgt, coarse_tgt, res):
        ref[...] = jnp.zeros(ref.shape, ref.dtype)
    level(
        fine_pairs, fine_classes, table, fine_stack, fine_flip, fine_out, fine_tgt, res,
        place * members * cf, cf, (members, members), 3 * members * cf,
    )
    level(
        coarse_pairs, coarse_classes, table, coarse_stack, coarse_flip, coarse_out, coarse_tgt,
        res, place * members * cc, LANES, (0, coarse_stack.shape[0]), 3 * members * cc,
    )
    fine_out[...] = fine_out[...] * sign_f
    fine_out[members : 2 * members] += fine_tgt[...]
    coarse_out[...] = coarse_out[...] * sign_f + coarse_tgt[...]


def from_behind(shard, axis, by):
    size = lax.axis_size(axis)
    pairs = [(i, i + by) for i in range(size) if 0 <= i + by < size]
    return lax.ppermute(shard, axis, pairs)


def per_device(fine_moments, coarse_moments, m2l_table, fine_pairs, coarse_pairs):
    k, cf = fine_moments.shape
    cc = coarse_moments.shape[1]
    members = lax.axis_size("sub") * lax.axis_size("lane")
    slots = 3 * members
    mine = jnp.concatenate([fine_moments, coarse_moments], axis=1)
    mine = jnp.pad(mine, ((0, ROWS - k), (0, LANES - cf - cc)))
    group = lax.all_gather(mine, ("sub", "lane"), axis=0, tiled=False)
    fine_stack = jnp.concatenate(
        [from_behind(group, "space", 1), group, from_behind(group, "space", -1)], axis=0
    )
    coarse_wide = slots * cc
    coarse_slots = -(-coarse_wide // LANES)
    coarse_stack = fine_stack[:, :, cf : cf + cc].transpose(1, 0, 2).reshape(ROWS, coarse_wide)
    coarse_stack = jnp.pad(coarse_stack, ((0, 0), (0, coarse_slots * LANES - coarse_wide)))
    coarse_stack = coarse_stack.reshape(ROWS, coarse_slots, LANES).transpose(1, 0, 2)
    vmem = pl.BlockSpec(memory_space=pltpu.VMEM)
    smem = pl.BlockSpec(memory_space=pltpu.SMEM)
    fine_part, coarse_part = pl.pallas_call(
        functools.partial(compute, (cf, cc, members, "space")),
        out_shape=(
            jax.ShapeDtypeStruct((slots, ROWS, LANES), F32),
            jax.ShapeDtypeStruct((coarse_slots, ROWS, LANES), F32),
        ),
        in_specs=[vmem] * 5 + [smem] * 2,
        out_specs=(vmem, vmem),
        scratch_shapes=[
            pltpu.VMEM((slots, ROWS, LANES), BF16),
            pltpu.VMEM((coarse_slots, ROWS, LANES), BF16),
            pltpu.VMEM((members, ROWS, LANES), F32),
            pltpu.VMEM((coarse_slots, ROWS, LANES), F32),
            pltpu.VMEM((2, ROWS, STEP), F32),
        ],
        compiler_params=pltpu.CompilerParams(vmem_limit_bytes=48 * 1024 * 1024),
    )(fine_stack, coarse_stack, m2l_table, fine_pairs, coarse_pairs, fine_pairs, coarse_pairs)
    coarse_part = coarse_part.transpose(1, 0, 2).reshape(ROWS, coarse_slots * LANES)
    coarse_part = coarse_part[:, :coarse_wide].reshape(ROWS, slots, cc).transpose(1, 0, 2)
    part = jnp.concatenate([fine_part[:, :k, :cf], coarse_part[:, :k]], axis=2)
    middle = (
        part[members : 2 * members]
        + from_behind(part[:members], "space", -1)
        + from_behind(part[2 * members :], "space", 1)
    )
    local = lax.psum_scatter(middle, ("sub", "lane"), scatter_dimension=0, tiled=False)
    return local[:, :cf], local[:, cf:]


def solution(mesh):
    cells = P(None, ("runs", "space", "sub", "lane"))
    return jax.shard_map(
        per_device,
        mesh=mesh,
        in_specs=(cells, cells, P(), cells, cells),
        out_specs=(cells, cells),
        check_vma=False,
    )
```

time: 281 us -> 113 us (0.40)
  other arithmetic: 93.2 us -> 1.96 us
  local copies, waits for them, and re-layouts: 96.2 us -> 10.6 us
  Pallas kernels: 0 us -> 36.7 us
  waiting for transfers between devices: 51 us -> 30.8 us
  blocking collectives: 11.6 us -> 6.12 us
    scatter-add x2 -> x0, other arithmetic: 89.1 us -> none  [pair_terms(): return total.at[:, store].add(result.reshape(width, -1))]
    gather x4 -> x0, local copies, waits for them, and re-layouts: 62.1 us -> none  [the longest x2 55.8 us: pair_terms(): moments[:, fetch].reshape(width, nblocks, 2, BLK)]
    pallas_call x0 -> x1, Pallas kernels: none -> 36.7 us  [per_device(): pl.pallas_call(functools.partial(compute, (cf, cc, members, 'space')), ou...]
    reshape x6 -> x2, local copies, waits for them, and re-layouts: 21.7 us -> 0.33 us  [the longest x1 0.22 us: per_device(): coarse_part[:, :coarse_wide].reshape(ROWS, slots, cc).transpose(1, 0, 2)]
    reduce_scatter x2 -> x1, waiting for transfers between devices: 40.8 us -> 23.2 us  [per_device(): lax.psum_scatter(middle, ('sub', 'lane'), scatter_dimension=0, tiled=False)]
    all_gather x2 -> x1, blocking collectives: 11.6 us -> 6.12 us  [per_device(): group = lax.all_gather(mine, ('sub', 'lane'), axis=0, tiled=False)]
    ppermute x2 -> x0, starting transfers between devices: 5.28 us -> none  [the longest x1 3.2 us: with_halo(): lax.ppermute(lax.slice_in_dim(block, block.shape[dim] - width, None, axis...]
    ppermute x2 -> x4, starting transfers between devices: 5.3 us -> 10.6 us  [from_behind(): return lax.ppermute(shard, axis, pairs)]
  transfers between devices with their start and end apart: 6 -> 5, of which waited for: 4 -> 3; matrix products, arithmetic and copies ran while one was open for 6% -> 5% of each run, Pallas kernels for 0% -> 0%
where the time goes in v1:
time: 113 us; the launch traced here: 111 us
  Pallas kernels  36.7 us (32%)
  waiting for transfers between devices  30.8 us (27%)
  between operations  14.1 us (12%)
  starting transfers between devices  10.6 us (9%)
  local copies, waits for them, and re-layouts  10.6 us (9%)
  blocking collectives  6.12 us (5%)
  other arithmetic  1.96 us (2%)
    pallas_call x1, Pallas kernels, per_device(): pl.pallas_call(functools.partial(compute, (cf, cc, members, 'space')), ou...  36.7 us
    reduce_scatter x1, waiting for transfers between devices, per_device(): lax.psum_scatter(middle, ('sub', 'lane'), scatter_dimension=0, tiled=False)  23.2 us
    ppermute x4, starting transfers between devices, from_behind(): return lax.ppermute(shard, axis, pairs)  10.6 us
    unnamed x9, local copies, waits for them, and re-layouts  8.88 us
    ppermute x4, waiting for transfers between devices, from_behind(): return lax.ppermute(shard, axis, pairs)  7.57 us
    all_gather x1, blocking collectives, per_device(): group = lax.all_gather(mine, ('sub', 'lane'), axis=0, tiled=False)  6.12 us
  transfers between devices with their start and end apart: 5, of which 3 were waited for; matrix products, arithmetic and copies ran while one was open for 5% of the time, Pallas kernels for 0%

profile of v1, /device:TPU:13, one launch (start us, length us, event | category | flops | bytes accessed | tf_op | source)
XLA Modules:
  0.0 110.8 jit_solution(825654949387634066)
XLA Ops:
  7.2 0.0 reduce-scatter.2.cloned.1.call-start
  7.2 0.8 copy.12
  8.0 0.9 fusion.9
  8.9 6.1 %all-gather = bf16[384,256]{1,0:T(8,128)(2,1)S(1)} all-gather(bf16[96,256]{1,0:T(8,128)(2,1)S(1)} %fusion.9), channel_id=2, replica_groups=mesh['runs'=2,'space'=4,'sub'=2,'lane'=2] {'sub','lane'}, dimensions={0}, use_global_device_ids=true | all-gather | bytes 245760 | tf_op jit(solution)/shard_map/all_gather | solution.py:161
  15.0 2.1 %collective-permute-start.1 = (bf16[4,96,256]{2,1,0:T(8,128)(2,1)S(1)}, bf16[4,96,256]{2,1,0:T(8,128)(2,1)S(1)}, u32[]{:S(2)}, u32[]{:S(2)}) collective-permute-start(bf16[4,96,256]{2,1,0:T(8,128)(2,1)S(1)} %bitcast.14), channel_id=1, source_target_pairs={{4,0},{8,4},{12,8},{5,1},{9,5},{13,9},{6,2},{10,6},{14,10},{7,3},{... | collective-permute-start | bytes 589832 | tf_op jit(solution)/shard_map/ppermute | solution.py:151
  17.1 3.2 %collective-permute-start = (bf16[4,96,256]{2,1,0:T(8,128)(2,1)S(1)}, bf16[4,96,256]{2,1,0:T(8,128)(2,1)S(1)}, u32[]{:S(2)}, u32[]{:S(2)}) collective-permute-start(bf16[4,96,256]{2,1,0:T(8,128)(2,1)S(1)} %bitcast.15), channel_id=1, source_target_pairs={{0,4},{4,8},{8,12},{1,5},{5,9},{9,13},{2,6},{6,10},{10,14},{3,7},{... | collective-permute-start | bytes 589832 | tf_op jit(solution)/shard_map/ppermute | solution.py:151
  20.3 5.0 %copy.15.table = bf16[158,81,81]{2,1,0:T(8,128)(2,1)} copy(bf16[158,81,81]{2,0,1:T(8,128)(2,1)} %param.7) | data formatting | bytes 4146552 | tf_op args[2]
  25.3 0.0 copy-start.1
  25.3 0.0 copy-start.2
  25.3 0.0 collective-permute-done.1
  25.3 0.0 collective-permute-done
  25.3 0.1 pad_maximum_fusion.fine_stack
  25.4 0.1 slice_bitcast_fusion
  25.5 0.1 copy.13
  25.7 0.1 copy.14
  25.8 0.4 copy-done.1
  26.2 0.0 copy-done.2
  26.2 0.0 copy-start
  26.2 2.0 %copy-done = bf16[158,81,81]{2,1,0:T(8,128)(2,1)S(1)} copy-done((bf16[158,81,81]{2,1,0:T(8,128)(2,1)S(1)}, bf16[158,81,81]{2,1,0:T(8,128)(2,1)}, u32[]{:S(2)}) %copy-start) | copy-done | bytes 2073300
  28.2 36.7 %shard_map.68 = (f32[12,96,256]{2,1,0:T(8,128)S(1)}, f32[1,96,256]{2,1,0:T(8,128)S(1)}) custom-call(bf16[12,96,256]{2,1,0:T(8,128)(2,1)S(1)} %pad_maximum_fusion.fine_stack, bf16[1,96,256]{2,1,0:T(8,128)(2,1)S(1)} %pad_bitcast_fusion.coarse_stack, bf16[158,81,81]{2,1,0:T(8,128)(2,1)S(1)} %copy-done, s32[3,6144]{1,0:T(4,128)S(1)} %copy-done.1, ...), custom_call_target="tpu_custom_call" | custom-call | tf_op jit(solution)/shard_map/pallas_call | solution.py:172
  64.9 0.1 slice.28
  65.0 0.1 copy.16
  65.1 0.2 copy.17
  65.4 0.2 fusion
  65.5 2.1 %collective-permute-start.2 = (f32[4,81,208]{2,1,0:T(8,128)S(1)}, f32[4,81,208]{2,1,0:T(8,128)S(1)}, u32[]{:S(2)}, u32[]{:S(2)}) collective-permute-start(f32[4,81,208]{2,1,0:T(8,128)S(1)} %get-tuple-element.10), channel_id=1, source_target_pairs={{4,0},{8,4},{12,8},{5,1},{9,5},{13,9},{6,2},{10,6},{14,10},{7,3},{... | collective-permute-start | bytes 808712 | tf_op jit(solution)/shard_map/ppermute | solution.py:151
  67.6 3.2 %collective-permute-start.3 = (f32[4,81,208]{2,1,0:T(8,128)S(1)}, f32[4,81,208]{2,1,0:T(8,128)S(1)}, u32[]{:S(2)}, u32[]{:S(2)}) collective-permute-start(f32[4,81,208]{2,1,0:T(8,128)S(1)} %get-tuple-element.11), channel_id=1, source_target_pairs={{0,4},{4,8},{8,12},{1,5},{5,9},{9,13},{2,6},{6,10},{10,14},{3,7},{... | collective-permute-start | bytes 808712 | tf_op jit(solution)/shard_map/ppermute | solution.py:151
  70.8 5.8 %collective-permute-done.2 = f32[4,81,208]{2,1,0:T(8,128)S(1)} collective-permute-done((f32[4,81,208]{2,1,0:T(8,128)S(1)}, f32[4,81,208]{2,1,0:T(8,128)S(1)}, u32[]{:S(2)}, u32[]{:S(2)}) %collective-permute-start.2) | collective-permute-done | bytes 269600 | tf_op jit(solution)/shard_map/ppermute | solution.py:151
  76.7 1.7 %collective-permute-done.3 = f32[4,81,208]{2,1,0:T(8,128)S(1)} collective-permute-done((f32[4,81,208]{2,1,0:T(8,128)S(1)}, f32[4,81,208]{2,1,0:T(8,128)S(1)}, u32[]{:S(2)}, u32[]{:S(2)}) %collective-permute-start.3) | collective-permute-done | bytes 269600 | tf_op jit(solution)/shard_map/ppermute | solution.py:151
  78.4 0.9 fusion.3
  79.3 0.0 reduce-scatter.2.cloned.1.call-update
  79.3 23.2 %reduce-scatter.2.cloned.1.call-done = f32[1,81,208]{2,1,0:T(8,128)} async-done(((f32[4,81,208]{2,1,0:T(8,128)}), f32[1,81,208]{2,1,0:T(8,128)}) %reduce-scatter.2.cloned.1.call-update) | async-done | bytes 67408 | tf_op jit(solution)/shard_map/reduce_scatter | solution.py:197
  102.5 0.9 slice.44
  103.3 0.7 copy.18
  (2 shorter events, 0.1 us)
Async XLA Ops:
  7.2 95.3 %reduce-scatter.2.cloned.1.call-start = ((), (), s32[]{:S(2)}) async-start(), calls=%async_computation.1 | async-start | bytes 450560 | tf_op jit(solution)/shard_map/reduce_scatter | solution.py:197
  15.0 10.3 %collective-permute-start.1 = (bf16[4,96,256]{2,1,0:T(8,128)(2,1)S(1)}, bf16[4,96,256]{2,1,0:T(8,128)(2,1)S(1)}, u32[]{:S(2)}, u32[]{:S(2)}) collective-permute-start(bf16[4,96,256]{2,1,0:T(8,128)(2,1)S(1)} %bitcast.14), channel_id=1, source_target_pairs={{4,0},{8,4},{12,8},{5,1},{9,5},{13,9},{6,2},{10,6},{14,10},{7,3},{... | collective-permute-start | bytes 589832 | tf_op jit(solution)/shard_map/ppermute | solution.py:151
  17.1 8.2 %collective-permute-start = (bf16[4,96,256]{2,1,0:T(8,128)(2,1)S(1)}, bf16[4,96,256]{2,1,0:T(8,128)(2,1)S(1)}, u32[]{:S(2)}, u32[]{:S(2)}) collective-permute-start(bf16[4,96,256]{2,1,0:T(8,128)(2,1)S(1)} %bitcast.15), channel_id=1, source_target_pairs={{0,4},{4,8},{8,12},{1,5},{5,9},{9,13},{2,6},{6,10},{10,14},{3,7},{... | collective-permute-start | bytes 589832 | tf_op jit(solution)/shard_map/ppermute | solution.py:151
  25.3 0.9 copy-start.1
  25.3 0.9 copy-start.2
  26.2 2.0 %copy-start = (bf16[158,81,81]{2,1,0:T(8,128)(2,1)S(1)}, bf16[158,81,81]{2,1,0:T(8,128)(2,1)}, u32[]{:S(2)}) copy-start(bf16[158,81,81]{2,1,0:T(8,128)(2,1)} %copy.15.table) | copy-start | bytes 6219832
  65.5 11.1 %collective-permute-start.2 = (f32[4,81,208]{2,1,0:T(8,128)S(1)}, f32[4,81,208]{2,1,0:T(8,128)S(1)}, u32[]{:S(2)}, u32[]{:S(2)}) collective-permute-start(f32[4,81,208]{2,1,0:T(8,128)S(1)} %get-tuple-element.10), channel_id=1, source_target_pairs={{4,0},{8,4},{12,8},{5,1},{9,5},{13,9},{6,2},{10,6},{14,10},{7,3},{... | collective-permute-start | bytes 808712 | tf_op jit(solution)/shard_map/ppermute | solution.py:151
  67.6 10.8 %collective-permute-start.3 = (f32[4,81,208]{2,1,0:T(8,128)S(1)}, f32[4,81,208]{2,1,0:T(8,128)S(1)}, u32[]{:S(2)}, u32[]{:S(2)}) collective-permute-start(f32[4,81,208]{2,1,0:T(8,128)S(1)} %get-tuple-element.11), channel_id=1, source_target_pairs={{0,4},{4,8},{8,12},{1,5},{5,9},{9,13},{2,6},{6,10},{10,14},{3,7},{... | collective-permute-start | bytes 808712 | tf_op jit(solution)/shard_map/ppermute | solution.py:151
Sparse Core Ops, SparseCore 0:
  79.4 22.9 reduce-scatter.1

commit v2 on v1

v2 whole, which is shorter than its diff:
```python
import functools

import jax
import jax.numpy as jnp
from jax import lax
from jax.experimental import pallas as pl
from jax.experimental.pallas import tpu as pltpu
from jax.sharding import PartitionSpec as P

BLK = 128
STEP = 256
LANES = 256
ROWS = 96
F32 = jnp.float32
BF16 = jnp.bfloat16


def divider(width, limit):
    for shift in range(31):
        mul = -(-(1 << shift) // width)
        if all((w * mul) >> shift == w // width for w in range(limit)):
            break
    assert limit * mul < 2**31
    return lambda w: (w * mul) >> shift


def row_sign(rows, dtype):
    index = lax.broadcasted_iota(jnp.int32, (rows, 1), 0)
    degree = jnp.zeros((rows, 1), jnp.int32)
    for root in range(1, 17):
        degree = degree + jnp.where(index >= root * root, 1, 0)
    return (1 - 2 * (degree & 1)).astype(F32).astype(dtype)


def split(values):
    top = values.astype(BF16)
    return top, (values - top.astype(F32)).astype(BF16)


def one_hot(lo):
    index = lax.broadcasted_iota(jnp.int32, (LANES, STEP), 0)
    return jnp.where(index == lo, 1.0, 0.0).astype(BF16)


def pick(stack, hi, hot):
    count = stack.shape[0]
    height = stack.shape[1]
    block = stack[...].reshape(count * height, LANES)
    all_parts = jnp.dot(block, hot, preferred_element_type=F32)
    got = jnp.zeros((height, STEP), F32)
    for h in range(count):
        got = jnp.where(hi == h, all_parts[h * height : (h + 1) * height], got)
    return got


def put(acc, hi, hot, values):
    count = acc.shape[0]
    height = values.shape[0]
    top, rest = split(values)
    both = jnp.concatenate([top, rest], axis=1)
    hi2 = jnp.concatenate([hi, hi], axis=1)
    spread = jnp.concatenate(
        [
            both * jnp.where(hi2 == h, 1.0, 0.0).astype(BF16)
            for h in range(count)
        ],
        axis=0,
    )
    hot2 = jnp.concatenate([hot, hot], axis=1)
    total = lax.dot_general(
        spread, hot2, (((1,), (1,)), ((), ())), preferred_element_type=F32
    )
    acc[...] += total.reshape(count, height, LANES)


def level(
    pairs, classes, table, stack, flipped, acc_src, acc_tgt, res, offset, width, first, cells
):
    width_of = divider(width, cells)
    classes_count = table.shape[0]
    k = table.shape[1]

    def step(i, carry):
        base = pl.multiple_of(i * STEP, STEP)
        src = pairs[0:1, pl.ds(base, STEP)] - offset
        tgt = pairs[1:2, pl.ds(base, STEP)] - offset
        live = pairs[2:3, pl.ds(base, STEP)] < classes_count
        src_hi = width_of(src)
        tgt_hi = width_of(tgt)
        src_hot = one_hot(src - src_hi * width)
        tgt_hot = one_hot(tgt - tgt_hi * width)
        src_hi = jnp.where(live, src_hi, -1)
        tgt_hi = jnp.where(live, tgt_hi - first, -1)
        from_src = pick(stack, src_hi, src_hot)
        from_tgt = pick(flipped, tgt_hi, tgt_hot)
        for j in range(STEP // BLK):
            at = slice(j * BLK, (j + 1) * BLK)
            operand = jnp.concatenate([from_src[:, at], from_tgt[:, at]], axis=1).astype(BF16)
            kind = jnp.minimum(classes[2, base + j * BLK], classes_count - 1)
            moved = jnp.dot(table[kind], operand[:k], preferred_element_type=F32)
            res[0, :k, at] = moved[:, :BLK]
            res[1, :k, at] = moved[:, BLK:]
        put(acc_tgt, tgt_hi, tgt_hot, res[0])
        put(acc_src, src_hi, src_hot, res[1])
        return carry

    lax.fori_loop(0, pairs.shape[1] // STEP, step, 0)


def kernel(
    sizes,
    mine_hbm,
    table_hbm,
    fine_hbm,
    coarse_hbm,
    fine_out,
    coarse_out,
    window,
    fine_flip,
    coarse_stack,
    coarse_flip,
    part,
    coarse_part,
    fine_tgt,
    coarse_tgt,
    res,
    arrived,
    table,
    fine_pairs,
    coarse_pairs,
    fine_classes,
    coarse_classes,
    local_sems,
    send_in,
    recv_in,
    send_out,
    recv_out,
):
    cf, cc, subs, lanes, spaces = sizes
    members = subs * lanes
    k = fine_out.shape[0]
    rows = arrived.shape[1]
    space = lax.axis_index("space")
    me = lax.axis_index("sub") * lanes + lax.axis_index("lane")

    local = [
        pltpu.make_async_copy(source, target, local_sems.at[n])
        for n, (source, target) in enumerate(
            (
                (table_hbm, table),
                (fine_hbm, fine_pairs),
                (coarse_hbm, coarse_pairs),
                (fine_hbm, fine_classes),
                (coarse_hbm, coarse_classes),
            )
        )
    ]
    for copy in local:
        copy.start()

    def partners(act, away_first=True):
        for step in (-1, 1, 0) if away_first else (0, -1, 1):
            for member in range(members):
                there = space + step
                near = jnp.logical_and(there >= 0, there < spaces)
                if step == 0:
                    near = member != me
                target = {
                    "space": there,
                    "sub": jnp.int32(member // lanes),
                    "lane": jnp.int32(member % lanes),
                }
                theirs = (1 + step) * members + member
                ours = (1 - step) * members + me
                pl.when(near)(functools.partial(act, target, theirs, ours))

    barrier = pltpu.get_barrier_semaphore()

    def greet(target, theirs, ours):
        pl.semaphore_signal(
            barrier, inc=1, device_id=target, device_id_type=pl.DeviceIdType.MESH
        )

    partners(greet)
    window[pl.ds(members + me, 1)] = mine_hbm[...][None]
    for step in (-1, 1):
        there = space + step
        first = (1 + step) * members

        @pl.when(jnp.logical_not(jnp.logical_and(there >= 0, there < spaces)))
        def _():
            window[first : first + members] = jnp.zeros((members, ROWS, LANES), BF16)

    beside = jnp.where(space > 0, 1, 0) + jnp.where(space < spaces - 1, 1, 0)
    pl.semaphore_wait(barrier, members - 1 + members * beside)

    def give(target, theirs, ours):
        return pltpu.make_async_remote_copy(
            src_ref=mine_hbm,
            dst_ref=window.at[ours],
            send_sem=send_in.at[theirs],
            recv_sem=recv_in.at[ours],
            device_id=target,
            device_id_type=pl.DeviceIdType.MESH,
        )

    def take(target, theirs, ours):
        return pltpu.make_async_remote_copy(
            src_ref=mine_hbm,
            dst_ref=window.at[theirs],
            send_sem=send_in.at[theirs],
            recv_sem=recv_in.at[theirs],
            device_id=target,
            device_id_type=pl.DeviceIdType.MESH,
        )

    partners(lambda *at: give(*at).start())
    for ref in (part, coarse_part, fine_tgt, coarse_tgt, res):
        ref[...] = jnp.zeros(ref.shape, ref.dtype)
    coarse_stack[...] = jnp.zeros(coarse_stack.shape, BF16)
    partners(lambda *at: take(*at).wait_recv())
    partners(lambda *at: give(*at).wait_send())

    sign_b = row_sign(ROWS, BF16)
    sign_f = row_sign(ROWS, F32)
    fine_flip[...] = window[members : 2 * members] * sign_b
    for slot in range(3 * members):
        h, at = divmod(slot * cc, LANES)
        coarse_stack[h, :, at : at + cc] = window[slot, :, cf : cf + cc]
    coarse_flip[...] = coarse_stack[...] * sign_b
    for copy in local:
        copy.wait()
    place = space - 1
    level(
        coarse_pairs, coarse_classes, table, coarse_stack, coarse_flip, coarse_part, coarse_tgt,
        res, place * members * cc, LANES, 0, 3 * members * cc,
    )
    level(
        fine_pairs, fine_classes, table, window, fine_flip, part, fine_tgt, res,
        place * members * cf, cf, members, 3 * members * cf,
    )
    coarse_part[...] = coarse_part[...] * sign_f + coarse_tgt[...]
    for slot in range(3 * members):
        h, at = divmod(slot * cc, LANES)
        total = part[slot] * sign_f
        if members <= slot < 2 * members:
            total = total + fine_tgt[slot - members]
        part[slot] = total
        part[slot, :, cf : cf + cc] = coarse_part[h, :, at : at + cc]

    def hand(target, theirs, ours):
        return pltpu.make_async_remote_copy(
            src_ref=part.at[theirs, 0:rows],
            dst_ref=arrived.at[ours],
            send_sem=send_out.at[theirs],
            recv_sem=recv_out.at[ours],
            device_id=target,
            device_id_type=pl.DeviceIdType.MESH,
        )

    def catch(target, theirs, ours):
        return pltpu.make_async_remote_copy(
            src_ref=part.at[theirs, 0:rows],
            dst_ref=arrived.at[theirs],
            send_sem=send_out.at[theirs],
            recv_sem=recv_out.at[theirs],
            device_id=target,
            device_id_type=pl.DeviceIdType.MESH,
        )

    partners(lambda *at: hand(*at).start())
    res[0, :rows] = part[pl.ds(members + me, 1), 0:rows][0]

    def gather(target, theirs, ours):
        catch(target, theirs, ours).wait_recv()
        res[0, :rows] += arrived[theirs]

    partners(gather, away_first=False)
    fine_out[...] = res[0, :k, :cf]
    coarse_out[...] = res[0, :k, cf : cf + cc]
    partners(lambda *at: hand(*at).wait_send())


def per_device(spaces, fine_moments, coarse_moments, m2l_table, fine_pairs, coarse_pairs):
    k, cf = fine_moments.shape
    cc = coarse_moments.shape[1]
    subs, lanes = lax.axis_size("sub"), lax.axis_size("lane")
    members = subs * lanes
    slots = 3 * members
    rows = -(-k // 8) * 8
    coarse_slots = -(-slots * cc // LANES)
    mine = jnp.concatenate([fine_moments, coarse_moments], axis=1)
    mine = jnp.pad(mine, ((0, ROWS - k), (0, LANES - cf - cc)))
    vmem = pl.BlockSpec(memory_space=pltpu.VMEM)
    anywhere = pl.BlockSpec(memory_space=pl.ANY)
    return pl.pallas_call(
        functools.partial(kernel, (cf, cc, subs, lanes, spaces)),
        out_shape=(
            jax.ShapeDtypeStruct((k, cf), F32),
            jax.ShapeDtypeStruct((k, cc), F32),
        ),
        in_specs=[vmem, anywhere, anywhere, anywhere],
        out_specs=(vmem, vmem),
        scratch_shapes=[
            pltpu.VMEM((slots, ROWS, LANES), BF16),
            pltpu.VMEM((members, ROWS, LANES), BF16),
            pltpu.VMEM((coarse_slots, ROWS, LANES), BF16),
            pltpu.VMEM((coarse_slots, ROWS, LANES), BF16),
            pltpu.VMEM((slots, ROWS, LANES), F32),
            pltpu.VMEM((coarse_slots, ROWS, LANES), F32),
            pltpu.VMEM((members, ROWS, LANES), F32),
            pltpu.VMEM((coarse_slots, ROWS, LANES), F32),
            pltpu.VMEM((2, ROWS, STEP), F32),
            pltpu.VMEM((slots, rows, LANES), F32),
            pltpu.VMEM(m2l_table.shape, BF16),
            pltpu.VMEM(fine_pairs.shape, jnp.int32),
            pltpu.VMEM(coarse_pairs.shape, jnp.int32),
            pltpu.SMEM(fine_pairs.shape, jnp.int32),
            pltpu.SMEM(coarse_pairs.shape, jnp.int32),
            pltpu.SemaphoreType.DMA((5,)),
            pltpu.SemaphoreType.DMA((slots,)),
            pltpu.SemaphoreType.DMA((slots,)),
            pltpu.SemaphoreType.DMA((slots,)),
            pltpu.SemaphoreType.DMA((slots,)),
        ],
        compiler_params=pltpu.CompilerParams(
            vmem_limit_bytes=48 * 1024 * 1024, collective_id=0, has_side_effects=True
        ),
    )(mine, m2l_table, fine_pairs, coarse_pairs)


def solution(mesh):
    cells = P(None, ("runs", "space", "sub", "lane"))
    return jax.shard_map(
        functools.partial(per_device, mesh.shape["space"]),
        mesh=mesh,
        in_specs=(cells, cells, P(), cells, cells),
        out_specs=(cells, cells),
        check_vma=False,
    )
```

time: 113 us -> 65.7 us (0.58); the launches traced: 111 us -> 65.3 us
  waiting for transfers between devices: 30.8 us -> 0 us
  Pallas kernels: 36.7 us -> 58.3 us
  between operations: 14.1 us -> 0.68 us
  starting transfers between devices: 10.6 us -> 0 us
  blocking collectives: 6.12 us -> 0 us
  local copies, waits for them, and re-layouts: 10.6 us -> 5.4 us
    reduce_scatter x1 -> x0, waiting for transfers between devices: 23.2 us -> none  [per_device(): lax.psum_scatter(middle, ('sub', 'lane'), scatter_dimension=0, tiled=False)]
    pallas_call x1, Pallas kernels: 36.7 us -> 58.3 us  [per_device(): pl.pallas_call(functools.partial(kernel, (cf, cc, subs, lanes, spaces)),...]
    ppermute x4 -> x0, starting transfers between devices: 10.6 us -> none  [from_behind(): return lax.ppermute(shard, axis, pairs)]
    ppermute x4 -> x0, waiting for transfers between devices: 7.57 us -> none  [from_behind(): return lax.ppermute(shard, axis, pairs)]
    all_gather x1 -> x0, blocking collectives: 6.12 us -> none  [per_device(): group = lax.all_gather(mine, ('sub', 'lane'), axis=0, tiled=False)]
    unnamed x9 -> x7, local copies, waits for them, and re-layouts: 8.88 us -> 4.73 us
  transfers between devices with their start and end apart: 5 -> 0, of which waited for: 3 -> 0; matrix products, arithmetic and copies ran while one was open for 5% -> 0% of each run, Pallas kernels for 0% -> 0%
where the time goes in v2:
time: 65.7 us; the launch traced here: 65.3 us
  Pallas kernels  58.3 us (89%)
  local copies, waits for them, and re-layouts  5.4 us (8%)
  other arithmetic  0.87 us (1%)
  between operations  0.68 us (1%)
    pallas_call x1, Pallas kernels, per_device(): pl.pallas_call(functools.partial(kernel, (cf, cc, subs, lanes, spaces)),...  58.3 us
    unnamed x7, local copies, waits for them, and re-layouts  4.73 us

profile of v2, /device:TPU:13, one launch (start us, length us, event | category | flops | bytes accessed | tf_op | source)
XLA Modules:
  0.0 65.3 jit_solution(8859595525167768525)
XLA Ops:
  0.6 0.0 copy-start.1
  0.6 0.0 copy-start
  0.7 0.8 %copy.7 = bf16[81,16]{1,0:T(8,128)(2,1)S(1)} copy(bf16[81,16]{0,1:T(8,128)(2,1)} %param.6) | data formatting | bytes 5184 | tf_op args[1]
  1.5 0.9 %fusion.5.mine_hbm = bf16[96,256]{1,0:T(8,128)(2,1)S(1)} fusion(bf16[81,16]{1,0:T(8,128)(2,1)S(1)} %copy.7, bf16[81,192]{1,0:T(8,128)(2,1)} %param.5), kind=kLoop, calls=%fused_computation.7 | loop fusion | flops 270336 | bytes 82848 | tf_op jit(solution)/shard_map/concatenate | solution.py:292
  2.4 3.3 %copy.8.table_hbm = bf16[158,81,81]{2,1,0:T(8,128)(2,1)S(1)} copy(bf16[158,81,81]{2,0,1:T(8,128)(2,1)} %param.7) | data formatting | bytes 4146552 | tf_op args[2]
  5.6 0.0 copy-done.1
  5.6 0.0 copy-done
  5.6 58.3 %shard_map.68 = (f32[81,192]{1,0:T(8,128)S(1)}, f32[81,16]{1,0:T(8,128)S(1)}) custom-call(bf16[96,256]{1,0:T(8,128)(2,1)S(1)} %fusion.5.mine_hbm, bf16[158,81,81]{2,1,0:T(8,128)(2,1)S(1)} %copy.8.table_hbm, s32[3,6144]{1,0:T(4,128)S(1)} %copy-done, s32[3,2048]{1,0:T(4,128)S(1)} %copy-done.1), custom_call_target="tpu_custom_call" | custom-call | tf_op jit(solution)/shard_map/pallas_call | solution.py:296
  64.0 0.7 %copy.9 = f32[81,16]{0,1:T(8,128)} copy(f32[81,16]{1,0:T(8,128)S(1)} %get-tuple-element.3) | data formatting | bytes 10368 | tf_op jit(solution)/shard_map/pallas_call | solution.py:296
  64.6 0.6 copy.11
Async XLA Ops:
  0.6 5.0 %copy-start.1 = (s32[3,2048]{1,0:T(4,128)S(1)}, s32[3,2048]{1,0:T(4,128)}, u32[]{:S(2)}) copy-start(s32[3,2048]{1,0:T(4,128)} %coarse_hbm.1) | copy-start | bytes 73732
  0.6 5.0 %copy-start = (s32[3,6144]{1,0:T(4,128)S(1)}, s32[3,6144]{1,0:T(4,128)}, u32[]{:S(2)}) copy-start(s32[3,6144]{1,0:T(4,128)} %fine_hbm.1) | copy-start | bytes 221188

commit v3 on v2

v3 whole, which is shorter than its diff:
```python
import functools

import jax
import jax.numpy as jnp
from jax import lax
from jax.experimental import pallas as pl
from jax.experimental.pallas import tpu as pltpu
from jax.sharding import PartitionSpec as P

BLK = 128
STEP = 256
PUT = 512
LANES = 256
ROWS = 96
F32 = jnp.float32
BF16 = jnp.bfloat16


def divider(width, limit):
    for shift in range(31):
        mul = -(-(1 << shift) // width)
        if all((w * mul) >> shift == w // width for w in range(limit)):
            break
    assert limit * mul < 2**31
    return lambda w: (w * mul) >> shift


def row_sign(rows, dtype):
    index = lax.broadcasted_iota(jnp.int32, (rows, 1), 0)
    degree = jnp.zeros((rows, 1), jnp.int32)
    for root in range(1, 17):
        degree = degree + jnp.where(index >= root * root, 1, 0)
    return (1 - 2 * (degree & 1)).astype(F32).astype(dtype)


def split(values):
    top = values.astype(BF16)
    return top, (values - top.astype(F32)).astype(BF16)


def one_hot(lo):
    index = lax.broadcasted_iota(jnp.int32, (LANES, lo.shape[1]), 0)
    return jnp.where(index == lo, 1.0, 0.0).astype(BF16)


def pick(stack, hi, hot):
    count, height, _ = stack.shape
    block = stack[...].reshape(count * height, LANES)
    all_parts = jnp.dot(block, hot, preferred_element_type=F32)
    got = jnp.zeros((height, hi.shape[1]), F32)
    for h in range(count):
        got = jnp.where(hi == h, all_parts[h * height : (h + 1) * height], got)
    return got


def locate(cells, live, offset, width, first, limit):
    cells = cells - offset
    hi = divider(width, limit)(cells)
    return jnp.where(live, hi - first, -1), cells - hi * width


def translate(pairs, classes, table, stack, flipped, results, offset, width, first, limit):
    kinds = table.shape[0]
    k = table.shape[1]
    to_tgt, to_tgt_rest, to_src, to_src_rest = results

    def step(i, carry):
        base = pl.multiple_of(i * STEP, STEP)
        live = pairs[2:3, pl.ds(base, STEP)] < kinds
        src_hi, src_lo = locate(pairs[0:1, pl.ds(base, STEP)], live, offset, width, 0, limit)
        tgt_hi, tgt_lo = locate(pairs[1:2, pl.ds(base, STEP)], live, offset, width, first, limit)
        from_src = pick(stack, src_hi, one_hot(src_lo))
        from_tgt = pick(flipped, tgt_hi, one_hot(tgt_lo))
        for j in range(STEP // BLK):
            at = slice(j * BLK, (j + 1) * BLK)
            here = pl.ds(pl.multiple_of(base + j * BLK, BLK), BLK)
            operand = jnp.concatenate([from_src[:, at], from_tgt[:, at]], axis=1).astype(BF16)
            kind = jnp.minimum(classes[2, base + j * BLK], kinds - 1)
            moved = jnp.dot(table[kind], operand[:k], preferred_element_type=F32)
            top, rest = split(moved)
            to_tgt[:k, here] = top[:, :BLK]
            to_tgt_rest[:k, here] = rest[:, :BLK]
            to_src[:k, here] = top[:, BLK:]
            to_src_rest[:k, here] = rest[:, BLK:]
        return carry

    lax.fori_loop(0, pairs.shape[1] // STEP, step, 0, unroll=2)


def scatter(pairs, row, kinds, acc, starts, results, offset, width, limit):
    count, height, _ = acc.shape
    top, rest = results
    n = PUT

    def step(i, carry):
        at = pl.ds(pl.multiple_of(i * n, n), n)
        live = pairs[2:3, at] < kinds
        hi, lo = locate(pairs[row : row + 1, at], live, offset, width, 0, limit)
        hot = one_hot(lo)
        both = jnp.concatenate([top[:, at], rest[:, at]], axis=1)
        hi = jnp.concatenate([hi, hi], axis=1)
        spread = jnp.concatenate(
            [both * jnp.where(hi == h, 1.0, 0.0).astype(BF16) for h in starts], axis=0
        )
        total = lax.dot_general(
            spread,
            jnp.concatenate([hot, hot], axis=1),
            (((1,), (1,)), ((), ())),
            preferred_element_type=F32,
        )
        acc[...] += total.reshape(count, height, LANES)
        return carry

    lax.fori_loop(0, pairs.shape[1] // n, step, 0)


def kernel(
    sizes,
    fine_moments,
    coarse_moments,
    table_hbm,
    fine_hbm,
    coarse_hbm,
    fine_out,
    coarse_out,
    mine,
    window,
    fine_flip,
    coarse_stack,
    coarse_flip,
    away,
    home,
    coarse_src,
    coarse_tgt,
    fine_tgt,
    total,
    fine_results,
    coarse_results,
    arrived,
    table,
    fine_pairs,
    coarse_pairs,
    fine_classes,
    coarse_classes,
    local_sems,
    send_in,
    recv_in,
    send_out,
    recv_out,
):
    cf, cc, subs, lanes, spaces = sizes
    members = subs * lanes
    k = fine_out.shape[0]
    rows = arrived.shape[1]
    space = lax.axis_index("space")
    me = lax.axis_index("sub") * lanes + lax.axis_index("lane")

    local = [
        pltpu.make_async_copy(source, target, local_sems.at[n])
        for n, (source, target) in enumerate(
            (
                (table_hbm, table),
                (fine_hbm, fine_pairs),
                (coarse_hbm, coarse_pairs),
                (fine_hbm, fine_classes),
                (coarse_hbm, coarse_classes),
            )
        )
    ]
    for copy in local:
        copy.start()

    def partners(act, steps=(-1, 1, 0)):
        for step in steps:
            for member in range(members):
                there = space + step
                near = jnp.logical_and(there >= 0, there < spaces)
                if step == 0:
                    near = member != me
                target = {
                    "space": there,
                    "sub": jnp.int32(member // lanes),
                    "lane": jnp.int32(member % lanes),
                }
                theirs = (1 + step) * members + member
                ours = (1 - step) * members + me
                pl.when(near)(functools.partial(act, target, theirs, ours))

    barrier = pltpu.get_barrier_semaphore()

    def greet(target, theirs, ours):
        pl.semaphore_signal(
            barrier, inc=1, device_id=target, device_id_type=pl.DeviceIdType.MESH
        )

    partners(greet)
    mine[...] = jnp.zeros(mine.shape, BF16)
    mine[:k, :cf] = fine_moments[...]
    mine[:k, cf : cf + cc] = coarse_moments[...].astype(F32).T.astype(BF16)
    window[pl.ds(members + me, 1)] = mine[...][None]
    for step in (-1, 1):
        there = space + step
        first = (1 + step) * members

        @pl.when(jnp.logical_not(jnp.logical_and(there >= 0, there < spaces)))
        def _():
            window[first : first + members] = jnp.zeros((members, ROWS, LANES), BF16)

    beside = jnp.where(space > 0, 1, 0) + jnp.where(space < spaces - 1, 1, 0)
    pl.semaphore_wait(barrier, members - 1 + members * beside)

    def give(target, theirs, ours):
        return pltpu.make_async_remote_copy(
            src_ref=mine,
            dst_ref=window.at[ours],
            send_sem=send_in.at[theirs],
            recv_sem=recv_in.at[ours],
            device_id=target,
            device_id_type=pl.DeviceIdType.MESH,
        )

    def take(target, theirs, ours):
        return pltpu.make_async_remote_copy(
            src_ref=mine,
            dst_ref=window.at[theirs],
            send_sem=send_in.at[theirs],
            recv_sem=recv_in.at[theirs],
            device_id=target,
            device_id_type=pl.DeviceIdType.MESH,
        )

    partners(lambda *at: give(*at).start())
    for ref in (away, home, coarse_src, coarse_tgt, fine_tgt):
        ref[...] = jnp.zeros(ref.shape, ref.dtype)
    coarse_stack[...] = jnp.zeros(coarse_stack.shape, BF16)
    partners(lambda *at: take(*at).wait_recv())
    partners(lambda *at: give(*at).wait_send())

    sign_b = row_sign(ROWS, BF16)
    sign_f = row_sign(ROWS, F32)
    fine_flip[...] = window[members : 2 * members] * sign_b
    for slot in range(3 * members):
        h, at = divmod(slot * cc, LANES)
        coarse_stack[h, :, at : at + cc] = window[slot, :, cf : cf + cc]
    coarse_flip[...] = coarse_stack[...] * sign_b
    for copy in local:
        copy.wait()
    kinds = table.shape[0]
    fine_at = ((space - 1) * members * cf, cf)
    coarse_at = ((space - 1) * members * cc, LANES)
    fine_limit, coarse_limit = 3 * members * cf, 3 * members * cc
    fine_parts = [fine_results.at[n] for n in range(4)]
    coarse_parts = [coarse_results.at[n] for n in range(4)]
    translate(
        coarse_pairs, coarse_classes, table, coarse_stack, coarse_flip, coarse_parts,
        *coarse_at, 0, coarse_limit,
    )
    translate(
        fine_pairs, fine_classes, table, window, fine_flip, fine_parts,
        *fine_at, members, fine_limit,
    )
    coarse_slots = range(coarse_src.shape[0])
    scatter(
        coarse_pairs, 0, kinds, coarse_src, coarse_slots, coarse_parts[2:], *coarse_at,
        coarse_limit,
    )
    scatter(
        coarse_pairs, 1, kinds, coarse_tgt, coarse_slots, coarse_parts[:2], *coarse_at,
        coarse_limit,
    )
    coarse_src[...] = coarse_src[...] * sign_f + coarse_tgt[...]

    def finish(ref, at, slot, more=None):
        value = ref[at] * sign_f
        ref[at] = value if more is None else value + more
        h, lane = divmod(slot * cc, LANES)
        ref[at, :, cf : cf + cc] = coarse_src[h, :, lane : lane + cc]

    inside = list(range(members, 2 * members))
    outside = [slot for slot in range(3 * members) if slot not in inside]
    scatter(
        fine_pairs, 0, kinds, away, outside, fine_parts[2:], *fine_at, fine_limit
    )
    for at, slot in enumerate(outside):
        finish(away, at, slot)

    def source(theirs):
        if theirs in inside:
            return home.at[theirs - members, 0:rows]
        return away.at[outside.index(theirs), 0:rows]

    def hand(target, theirs, ours):
        return pltpu.make_async_remote_copy(
            src_ref=source(theirs),
            dst_ref=arrived.at[ours],
            send_sem=send_out.at[theirs],
            recv_sem=recv_out.at[ours],
            device_id=target,
            device_id_type=pl.DeviceIdType.MESH,
        )

    def catch(target, theirs, ours):
        return pltpu.make_async_remote_copy(
            src_ref=source(theirs),
            dst_ref=arrived.at[theirs],
            send_sem=send_out.at[theirs],
            recv_sem=recv_out.at[theirs],
            device_id=target,
            device_id_type=pl.DeviceIdType.MESH,
        )

    def gather(target, theirs, ours):
        catch(target, theirs, ours).wait_recv()
        total[...] += arrived[theirs]

    partners(lambda *at: hand(*at).start(), (-1, 1))
    scatter(
        fine_pairs, 0, kinds, home, inside, fine_parts[2:], *fine_at, fine_limit
    )
    scatter(
        fine_pairs, 1, kinds, fine_tgt, inside, fine_parts[:2], *fine_at, fine_limit
    )
    for at, slot in enumerate(inside):
        finish(home, at, slot, fine_tgt[at])
    partners(lambda *at: hand(*at).start(), (0,))
    total[...] = home[pl.ds(me, 1), 0:rows][0]
    partners(gather, (-1, 1))
    partners(gather, (0,))
    fine_out[...] = total[:k, :cf]
    coarse_out[...] = total[:, cf : cf + cc].T[:, :k]
    partners(lambda *at: hand(*at).wait_send())


def per_device(spaces, fine_moments, coarse_moments, m2l_table, fine_pairs, coarse_pairs):
    k, cf = fine_moments.shape
    cc = coarse_moments.shape[1]
    subs, lanes = lax.axis_size("sub"), lax.axis_size("lane")
    members = subs * lanes
    slots = 3 * members
    rows = -(-k // 8) * 8
    coarse_slots = -(-slots * cc // LANES)
    vmem = pl.BlockSpec(memory_space=pltpu.VMEM)
    anywhere = pl.BlockSpec(memory_space=pl.ANY)
    fine_local, coarse_local = pl.pallas_call(
        functools.partial(kernel, (cf, cc, subs, lanes, spaces)),
        out_shape=(
            jax.ShapeDtypeStruct((k, cf), F32),
            jax.ShapeDtypeStruct((cc, k), F32),
        ),
        in_specs=[vmem, vmem, anywhere, anywhere, anywhere],
        out_specs=(vmem, vmem),
        scratch_shapes=[
            pltpu.VMEM((ROWS, LANES), BF16),
            pltpu.VMEM((slots, ROWS, LANES), BF16),
            pltpu.VMEM((members, ROWS, LANES), BF16),
            pltpu.VMEM((coarse_slots, ROWS, LANES), BF16),
            pltpu.VMEM((coarse_slots, ROWS, LANES), BF16),
            pltpu.VMEM((2 * members, ROWS, LANES), F32),
            pltpu.VMEM((members, ROWS, LANES), F32),
            pltpu.VMEM((coarse_slots, ROWS, LANES), F32),
            pltpu.VMEM((coarse_slots, ROWS, LANES), F32),
            pltpu.VMEM((members, ROWS, LANES), F32),
            pltpu.VMEM((rows, LANES), F32),
            pltpu.VMEM((4, ROWS, fine_pairs.shape[1]), BF16),
            pltpu.VMEM((4, ROWS, coarse_pairs.shape[1]), BF16),
            pltpu.VMEM((slots, rows, LANES), F32),
            pltpu.VMEM(m2l_table.shape, BF16),
            pltpu.VMEM(fine_pairs.shape, jnp.int32),
            pltpu.VMEM(coarse_pairs.shape, jnp.int32),
            pltpu.SMEM(fine_pairs.shape, jnp.int32),
            pltpu.SMEM(coarse_pairs.shape, jnp.int32),
            pltpu.SemaphoreType.DMA((5,)),
            pltpu.SemaphoreType.DMA((slots,)),
            pltpu.SemaphoreType.DMA((slots,)),
            pltpu.SemaphoreType.DMA((slots,)),
            pltpu.SemaphoreType.DMA((slots,)),
        ],
        compiler_params=pltpu.CompilerParams(
            vmem_limit_bytes=48 * 1024 * 1024, collective_id=0, has_side_effects=True
        ),
    )(fine_moments, coarse_moments.T, m2l_table, fine_pairs, coarse_pairs)
    return fine_local, coarse_local.T


def solution(mesh):
    cells = P(None, ("runs", "space", "sub", "lane"))
    return jax.shard_map(
        functools.partial(per_device, mesh.shape["space"]),
        mesh=mesh,
        in_specs=(cells, cells, P(), cells, cells),
        out_specs=(cells, cells),
        check_vma=False,
    )
```

time: 65.7 us -> 59.5 us (0.906)
  Pallas kernels: 58.3 us -> 54.1 us
  other arithmetic: 0.87 us -> 0 us
  local copies, waits for them, and re-layouts: 5.4 us -> 4.56 us
    pallas_call x1, Pallas kernels: 58.3 us -> 54.1 us  [per_device(): pl.pallas_call(functools.partial(kernel, (cf, cc, subs, lanes, spaces)),...]
    concatenate x1 -> x0, other arithmetic: 0.87 us -> none  [per_device(): mine = jnp.concatenate([fine_moments, coarse_moments], axis=1)]
    pallas_call x1 -> x0, local copies, waits for them, and re-layouts: 0.67 us -> none  [per_device(): pl.pallas_call(functools.partial(kernel, (cf, cc, subs, lanes, spaces)),...]
    unnamed x7 -> x11, local copies, waits for them, and re-layouts: 4.73 us -> 4.56 us
where the time goes in v3:
time: 59.5 us; the launch traced here: 59.4 us
  Pallas kernels  54.1 us (91%)
  local copies, waits for them, and re-layouts  4.56 us (8%)
  between operations  0.71 us (1%)
    pallas_call x1, Pallas kernels, per_device(): pl.pallas_call(functools.partial(kernel, (cf, cc, subs, lanes, spaces)),...  54.1 us
    unnamed x11, local copies, waits for them, and re-layouts  4.56 us

profile of v3, /device:TPU:13, one launch (start us, length us, event | category | flops | bytes accessed | tf_op | source)
XLA Modules:
  0.0 59.4 jit_solution(7226779973813389589)
XLA Ops:
  0.6 0.0 copy-start.2
  0.6 0.0 copy-start
  0.7 0.0 copy-start.3
  0.7 0.0 copy-start.1
  0.7 3.3 %copy.7.table_hbm = bf16[158,81,81]{2,1,0:T(8,128)(2,1)S(1)} copy(bf16[158,81,81]{2,0,1:T(8,128)(2,1)} %param.7) | data formatting | bytes 4146552 | tf_op args[2]
  4.0 0.0 copy-done.2
  4.0 0.0 copy-done
  4.0 0.0 copy-done.3
  4.0 0.0 copy-done.1
  4.0 54.1 %shard_map.68 = (f32[81,192]{1,0:T(8,128)S(1)}, f32[16,81]{1,0:T(8,128)S(1)}) custom-call(bf16[81,192]{1,0:T(8,128)(2,1)S(1)} %copy-done.1, bf16[16,81]{1,0:T(8,128)(2,1)S(1)} %bitcast.3, bf16[158,81,81]{2,1,0:T(8,128)(2,1)S(1)} %copy.7.table_hbm, s32[3,6144]{1,0:T(4,128)S(1)} %copy-done, s32[3,2048]{1,0:T(4,128)S(1)} %copy-done.2), custom_call_target="tpu_custom_call" | custom-call | tf_op jit(solution)/shard_map/pallas_call | solution.py:344
  58.2 0.6 %copy.10 = f32[81,192]{1,0:T(8,128)} copy(f32[81,192]{1,0:T(8,128)S(1)} %get-tuple-element.8) | data formatting | bytes 124416
  58.8 0.6 %copy.11 = f32[81,16]{0,1:T(8,128)} copy(f32[81,16]{0,1:T(8,128)S(1)} %bitcast.2) | data formatting | bytes 10368
Async XLA Ops:
  0.6 3.4 %copy-start.2 = (s32[3,2048]{1,0:T(4,128)S(1)}, s32[3,2048]{1,0:T(4,128)}, u32[]{:S(2)}) copy-start(s32[3,2048]{1,0:T(4,128)} %coarse_hbm.1) | copy-start | bytes 73732
  0.6 3.4 %copy-start = (s32[3,6144]{1,0:T(4,128)S(1)}, s32[3,6144]{1,0:T(4,128)}, u32[]{:S(2)}) copy-start(s32[3,6144]{1,0:T(4,128)} %fine_hbm.1) | copy-start | bytes 221188
  0.7 3.4 %copy-start.3 = (bf16[81,16]{0,1:T(8,128)(2,1)S(1)}, bf16[81,16]{0,1:T(8,128)(2,1)}, u32[]{:S(2)}) copy-start(bf16[81,16]{0,1:T(8,128)(2,1)} %param.6) | copy-start | bytes 7780
  0.7 3.4 %copy-start.1 = (bf16[81,192]{1,0:T(8,128)(2,1)S(1)}, bf16[81,192]{1,0:T(8,128)(2,1)}, u32[]{:S(2)}) copy-start(bf16[81,192]{1,0:T(8,128)(2,1)} %fine_moments.1) | copy-start | bytes 93316

commit v4 on v3

--- a/solution.py
+++ b/solution.py
@@ -8,8 +8,9 @@
 from jax.sharding import PartitionSpec as P
 
 BLK = 128
-STEP = 256
-PUT = 512
+STEP = 512
+PUT = 1024
+UNROLL = 2
 LANES = 256
 ROWS = 96
 F32 = jnp.float32
@@ -59,7 +60,18 @@
     return jnp.where(live, hi - first, -1), cells - hi * width
 
 
-def translate(pairs, classes, table, stack, flipped, results, offset, width, first, limit):
+def fetch_targets(pairs, kinds, flipped, fetched, offset, width, first, limit):
+    def step(i, carry):
+        at = pl.ds(pl.multiple_of(i * STEP, STEP), STEP)
+        live = pairs[2:3, at] < kinds
+        hi, lo = locate(pairs[1:2, at], live, offset, width, first, limit)
+        fetched[:, at] = pick(flipped, hi, one_hot(lo)).astype(BF16)
+        return carry
+
+    lax.fori_loop(0, pairs.shape[1] // STEP, step, 0, unroll=UNROLL)
+
+
+def translate(pairs, classes, table, stack, fetched, results, offset, width, limit):
     kinds = table.shape[0]
     k = table.shape[1]
     to_tgt, to_tgt_rest, to_src, to_src_rest = results
@@ -68,13 +80,12 @@
         base = pl.multiple_of(i * STEP, STEP)
         live = pairs[2:3, pl.ds(base, STEP)] < kinds
         src_hi, src_lo = locate(pairs[0:1, pl.ds(base, STEP)], live, offset, width, 0, limit)
-        tgt_hi, tgt_lo = locate(pairs[1:2, pl.ds(base, STEP)], live, offset, width, first, limit)
-        from_src = pick(stack, src_hi, one_hot(src_lo))
-        from_tgt = pick(flipped, tgt_hi, one_hot(tgt_lo))
+        from_src = pick(stack, src_hi, one_hot(src_lo)).astype(BF16)
+        from_tgt = fetched[:, pl.ds(base, STEP)]
         for j in range(STEP // BLK):
             at = slice(j * BLK, (j + 1) * BLK)
             here = pl.ds(pl.multiple_of(base + j * BLK, BLK), BLK)
-            operand = jnp.concatenate([from_src[:, at], from_tgt[:, at]], axis=1).astype(BF16)
+            operand = jnp.concatenate([from_src[:, at], from_tgt[:, at]], axis=1)
             kind = jnp.minimum(classes[2, base + j * BLK], kinds - 1)
             moved = jnp.dot(table[kind], operand[:k], preferred_element_type=F32)
             top, rest = split(moved)
@@ -84,7 +95,7 @@
             to_src_rest[:k, here] = rest[:, BLK:]
         return carry
 
-    lax.fori_loop(0, pairs.shape[1] // STEP, step, 0, unroll=2)
+    lax.fori_loop(0, pairs.shape[1] // STEP, step, 0, unroll=UNROLL)
 
 
 def scatter(pairs, row, kinds, acc, starts, results, offset, width, limit):
@@ -134,6 +145,8 @@
     coarse_tgt,
     fine_tgt,
     total,
+    fine_fetched,
+    coarse_fetched,
     fine_results,
     coarse_results,
     arrived,
@@ -229,35 +242,41 @@
             device_id_type=pl.DeviceIdType.MESH,
         )
 
-    partners(lambda *at: give(*at).start())
+    partners(lambda *at: give(*at).start(), (0, -1, 1))
     for ref in (away, home, coarse_src, coarse_tgt, fine_tgt):
         ref[...] = jnp.zeros(ref.shape, ref.dtype)
     coarse_stack[...] = jnp.zeros(coarse_stack.shape, BF16)
-    partners(lambda *at: take(*at).wait_recv())
-    partners(lambda *at: give(*at).wait_send())
-
     sign_b = row_sign(ROWS, BF16)
     sign_f = row_sign(ROWS, F32)
+    kinds = table.shape[0]
+    fine_at = ((space - 1) * members * cf, cf)
+    coarse_at = ((space - 1) * members * cc, LANES)
+    fine_limit, coarse_limit = 3 * members * cf, 3 * members * cc
+    partners(lambda *at: take(*at).wait_recv(), (0,))
     fine_flip[...] = window[members : 2 * members] * sign_b
+    for copy in local:
+        copy.wait()
+    fetch_targets(
+        fine_pairs, kinds, fine_flip, fine_fetched, *fine_at, members, fine_limit
+    )
+    partners(lambda *at: take(*at).wait_recv(), (-1, 1))
+    partners(lambda *at: give(*at).wait_send())
     for slot in range(3 * members):
         h, at = divmod(slot * cc, LANES)
         coarse_stack[h, :, at : at + cc] = window[slot, :, cf : cf + cc]
     coarse_flip[...] = coarse_stack[...] * sign_b
-    for copy in local:
-        copy.wait()
-    kinds = table.shape[0]
-    fine_at = ((space - 1) * members * cf, cf)
-    coarse_at = ((space - 1) * members * cc, LANES)
-    fine_limit, coarse_limit = 3 * members * cf, 3 * members * cc
+    fetch_targets(
+        coarse_pairs, kinds, coarse_flip, coarse_fetched, *coarse_at, 0, coarse_limit
+    )
     fine_parts = [fine_results.at[n] for n in range(4)]
     coarse_parts = [coarse_results.at[n] for n in range(4)]
     translate(
-        coarse_pairs, coarse_classes, table, coarse_stack, coarse_flip, coarse_parts,
-        *coarse_at, 0, coarse_limit,
+        coarse_pairs, coarse_classes, table, coarse_stack, coarse_fetched, coarse_parts,
+        *coarse_at, coarse_limit,
     )
     translate(
-        fine_pairs, fine_classes, table, window, fine_flip, fine_parts,
-        *fine_at, members, fine_limit,
+        fine_pairs, fine_classes, table, window, fine_fetched, fine_parts,
+        *fine_at, fine_limit,
     )
     coarse_slots = range(coarse_src.shape[0])
     scatter(
@@ -361,6 +380,8 @@
             pltpu.VMEM((coarse_slots, ROWS, LANES), F32),
             pltpu.VMEM((members, ROWS, LANES), F32),
             pltpu.VMEM((rows, LANES), F32),
+            pltpu.VMEM((ROWS, fine_pairs.shape[1]), BF16),
+            pltpu.VMEM((ROWS, coarse_pairs.shape[1]), BF16),
             pltpu.VMEM((4, ROWS, fine_pairs.shape[1]), BF16),
             pltpu.VMEM((4, ROWS, coarse_pairs.shape[1]), BF16),
             pltpu.VMEM((slots, rows, LANES), F32),

time: 59.5 us -> 52 us (0.87)
  the two profiles are of different devices: /device:TPU:13 before, /device:TPU:19 now
where the time goes in v4:
time: 52 us; the launch traced here: 51.9 us
  Pallas kernels  46.6 us (90%)
  local copies, waits for them, and re-layouts  4.56 us (9%)
  between operations  0.71 us (1%)
    pallas_call x1, Pallas kernels, per_device(): pl.pallas_call(functools.partial(kernel, (cf, cc, subs, lanes, spaces)),...  46.6 us
    unnamed x11, local copies, waits for them, and re-layouts  4.56 us

profile of v4, /device:TPU:19, one launch (start us, length us, event | category | flops | bytes accessed | tf_op | source)
XLA Modules:
  0.0 51.9 jit_solution(5841328079059004797)
XLA Ops:
  0.6 0.0 copy-start.2
  0.6 0.0 copy-start
  0.7 0.0 copy-start.3
  0.7 0.0 copy-start.1
  0.7 3.3 %copy.7.table_hbm = bf16[158,81,81]{2,1,0:T(8,128)(2,1)S(1)} copy(bf16[158,81,81]{2,0,1:T(8,128)(2,1)} %param.7) | data formatting | bytes 4146552 | tf_op args[2]
  4.0 0.0 copy-done.2
  4.0 0.0 copy-done
  4.0 0.0 copy-done.3
  4.0 0.0 copy-done.1
  4.0 46.6 %shard_map.68 = (f32[81,192]{1,0:T(8,128)S(1)}, f32[16,81]{1,0:T(8,128)S(1)}) custom-call(bf16[81,192]{1,0:T(8,128)(2,1)S(1)} %copy-done.1, bf16[16,81]{1,0:T(8,128)(2,1)S(1)} %bitcast.3, bf16[158,81,81]{2,1,0:T(8,128)(2,1)S(1)} %copy.7.table_hbm, s32[3,6144]{1,0:T(4,128)S(1)} %copy-done, s32[3,2048]{1,0:T(4,128)S(1)} %copy-done.2), custom_call_target="tpu_custom_call" | custom-call | tf_op jit(solution)/shard_map/pallas_call | solution.py:363
  50.6 0.6 %copy.10 = f32[81,192]{1,0:T(8,128)} copy(f32[81,192]{1,0:T(8,128)S(1)} %get-tuple-element.8) | data formatting | bytes 124416
  51.3 0.6 %copy.11 = f32[81,16]{0,1:T(8,128)} copy(f32[81,16]{0,1:T(8,128)S(1)} %bitcast.2) | data formatting | bytes 10368
Async XLA Ops:
  0.6 3.4 %copy-start.2 = (s32[3,2048]{1,0:T(4,128)S(1)}, s32[3,2048]{1,0:T(4,128)}, u32[]{:S(2)}) copy-start(s32[3,2048]{1,0:T(4,128)} %coarse_hbm.1) | copy-start | bytes 73732
  0.6 3.4 %copy-start = (s32[3,6144]{1,0:T(4,128)S(1)}, s32[3,6144]{1,0:T(4,128)}, u32[]{:S(2)}) copy-start(s32[3,6144]{1,0:T(4,128)} %fine_hbm.1) | copy-start | bytes 221188
  0.7 3.4 %copy-start.3 = (bf16[81,16]{0,1:T(8,128)(2,1)S(1)}, bf16[81,16]{0,1:T(8,128)(2,1)}, u32[]{:S(2)}) copy-start(bf16[81,16]{0,1:T(8,128)(2,1)} %param.6) | copy-start | bytes 7780
  0.7 3.4 %copy-start.1 = (bf16[81,192]{1,0:T(8,128)(2,1)S(1)}, bf16[81,192]{1,0:T(8,128)(2,1)}, u32[]{:S(2)}) copy-start(bf16[81,192]{1,0:T(8,128)(2,1)} %fine_moments.1) | copy-start | bytes 93316
